TPU v7x, 32 devices: a whole 2x2x4 slice. The times are simulated.
32 devices in a mesh: ctx: 16 (over z, y, x), head: 2 (over core).
Axes of the slice: x: 2, y: 2, z: 4, core: 2. Of those that a mesh axis runs over, the one named last changes fastest.
Arguments:
- queries: bfloat16 [2048, 4096], P('ctx', 'head'), may hold values from -30 to 30
- keys: bfloat16 [8, 2048, 1024], P(None, 'ctx', 'head'), may hold values from -12 to 12
- values: bfloat16 [8, 2048, 1024], P(None, 'ctx', 'head'), may hold values from -6 to 6
- out_weight: bfloat16 [4096, 4096], P('head'), may hold values from -0.09375 to 0.09375
- vertical: int32 [8, 8], P('head'), may hold values from 0 to 111, as said below
- slash: int32 [8, 8], P('head'), may hold values from 1 to 112, as said below
Outputs:
- mixed: bfloat16 [2048, 4096], P('ctx', 'head')
Inputs may be any that keep to these rules, and one draw needn't show every extreme that they name: `vertical`: for each key-value head the 8 entries have distinct residues modulo 16, and all lie before block (7) * 16. `slash`: for each key-value head the 8 offsets have distinct residues modulo 16.
All inputs are finite; a program needn't handle non-finite values.
Results may differ from a plain program's by a relative error of at most 0.02.
Values may be sent and summed in bfloat16 or wider, within the bound.
A program may use at most 128 MiB of HBM per device.

v0:
```python
import jax
import jax.numpy as jnp
from jax import lax
from jax.sharding import PartitionSpec as P

H = 32
KVH = 8
HD = 128


NEGATIVE = -1e30


def absorb(state, scores, values_tile, form):
    running_max, running_sum, weighted = state
    new_max = jnp.maximum(running_max, jnp.max(scores, axis=(2, 3)))
    shrink = jnp.exp(running_max - new_max)
    weights = jnp.exp(scores - new_max[:, :, None, None])
    running_sum = running_sum * shrink + jnp.sum(weights, axis=(2, 3))
    weighted = weighted * shrink[:, :, None] + jnp.einsum(
        form, weights.astype(jnp.bfloat16), values_tile, preferred_element_type=jnp.float32
    )
    return (new_max, running_sum, weighted)


def per_device(queries, keys, values, out_weight, vertical, slash):
    shards = lax.axis_size("ctx")
    own_index = lax.axis_index("ctx")
    groups = vertical.shape[0]
    rounds = keys.shape[0]
    block = queries.shape[0]
    heads_per = H // KVH
    row_count = heads_per * block
    factor = HD ** (-0.5)
    key_local = keys.reshape(rounds, block, groups, HD)
    value_local = values.reshape(rounds, block, groups, HD)
    query_rows = (
        queries.reshape(block, groups, heads_per, HD)
        .transpose(1, 2, 0, 3)
        .reshape(groups, row_count, HD)
    )
    residue_v = vertical % shards
    holding = residue_v == own_index
    has_vertical = jnp.any(holding, axis=1)
    round_v = jnp.sum(jnp.where(holding, vertical // shards, 0), axis=1)
    slot_keys = jnp.stack(
        [key_local[round_v[group_index], :, group_index, :] for group_index in range(groups)]
    )
    slot_values = jnp.stack(
        [value_local[round_v[group_index], :, group_index, :] for group_index in range(groups)]
    )
    slot_keys = jnp.where(has_vertical[:, None, None], slot_keys, jnp.zeros_like(slot_keys))[None]
    slot_values = jnp.where(has_vertical[:, None, None], slot_values, jnp.zeros_like(slot_values))[
        None
    ]
    initial = (
        jnp.full((groups, row_count), NEGATIVE, jnp.float32),
        jnp.zeros((groups, row_count), jnp.float32),
        jnp.zeros((groups, row_count, HD), jnp.float32),
    )
    piece_keys = lax.all_gather(slot_keys, "ctx", axis=0, tiled=True)
    piece_values = lax.all_gather(slot_values, "ctx", axis=0, tiled=True)
    owners = jnp.arange(piece_keys.shape[0], dtype=jnp.int32)
    present = jnp.any(residue_v[:, None, :] == owners[None, :, None], axis=2)
    scores = (
        jnp.einsum("grd,ngkd->grnk", query_rows, piece_keys, preferred_element_type=jnp.float32)
        * factor
    )
    scores = jnp.where(present[:, None, :, None], scores, -jnp.inf)
    state = absorb(initial, scores, piece_values, "grnk,ngkd->grd")
    own_keys = key_local[rounds - 1]
    own_values = value_local[rounds - 1].transpose(1, 0, 2)[:, None]
    own_scores = (
        jnp.einsum("grd,kgd->grk", query_rows, own_keys, preferred_element_type=jnp.float32)
        * factor
    )
    query_place = jnp.arange(row_count) % block
    causal = query_place[:, None] >= jnp.arange(block)[None, :]
    own_scores = jnp.where(causal[None], own_scores, -jnp.inf)[:, :, None, :]
    state = absorb(state, own_scores, own_values, "grnk,gnkd->grd")
    last_base = (rounds - 1) * shards
    residue_s = slash % shards
    targets = jnp.arange(shards, dtype=jnp.int32)
    wanted = (targets - own_index) % shards
    matching = residue_s[:, None, :] == wanted[None, :, None]
    chosen = jnp.sum(jnp.where(matching, slash[:, None, :], 0), axis=2)
    source_round = (last_base + targets[None, :] - chosen) // shards
    send_keys = jnp.stack(
        [
            jnp.take(key_local[:, :, group_index, :], source_round[group_index], axis=0)
            for group_index in range(groups)
        ],
        axis=1,
    )
    send_values = jnp.stack(
        [
            jnp.take(value_local[:, :, group_index, :], source_round[group_index], axis=0)
            for group_index in range(groups)
        ],
        axis=1,
    )
    got_keys, got_values = (
        lax.all_to_all(send_keys, "ctx", split_axis=0, concat_axis=0, tiled=True),
        lax.all_to_all(send_values, "ctx", split_axis=0, concat_axis=0, tiled=True),
    )
    anchor = (own_index - residue_s) % shards
    item_keys = jnp.stack(
        [
            jnp.take(got_keys[:, group_index], anchor[group_index], axis=0)
            for group_index in range(groups)
        ]
    )
    item_values = jnp.stack(
        [
            jnp.take(got_values[:, group_index], anchor[group_index], axis=0)
            for group_index in range(groups)
        ]
    )
    slash_blocks = last_base + own_index - slash
    repeated = jnp.any(slash_blocks[:, :, None] == vertical[:, None, :], axis=2)
    item_scores = (
        jnp.einsum("grd,gikd->grik", query_rows, item_keys, preferred_element_type=jnp.float32)
        * factor
    )
    item_scores = jnp.where(jnp.logical_not(repeated)[:, None, :, None], item_scores, -jnp.inf)
    state = absorb(state, item_scores, item_values, "grnk,gnkd->grd")
    running_max, running_sum, weighted = state
    attended = weighted / running_sum[:, :, None]
    attended = (
        attended.reshape(groups, heads_per, block, HD)
        .transpose(2, 0, 1, 3)
        .reshape(block, groups * heads_per * HD)
        .astype(jnp.bfloat16)
    )
    terms = jnp.dot(attended, out_weight, preferred_element_type=jnp.float32)
    return lax.psum_scatter(terms.astype(jnp.bfloat16), "head", scatter_dimension=1, tiled=True)


def solution(mesh):
    in_specs = (
        P("ctx", "head"),
        P(None, "ctx", "head"),
        P(None, "ctx", "head"),
        P("head", None),
        P("head", None),
        P("head", None),
    )
    out_specs = P("ctx", "head")
    return jax.shard_map(
        per_device, mesh=mesh, in_specs=in_specs, out_specs=out_specs, check_vma=False
    )
```

profile of v0, /device:TPU:0, one launch (start us, length us, event | category | flops | bytes accessed | tf_op | source)
XLA Modules:
  0.0 252.6 jit_solution(7814776050583881501)
XLA Ops:
  7.4 1.6 copy.90
  11.7 1.6 copy.84
  30.9 2.0 select_bitcast_fusion
  32.9 2.2 select_bitcast_fusion.1
  35.1 2.1 select_bitcast_fusion.2
  37.2 2.1 select_bitcast_fusion.3
  41.1 8.3 %all-to-all-start.1 = ((bf16[16,4,128,128]{3,2,1,0:T(8,128)(2,1)}), bf16[16,4,128,128]{3,2,1,0:T(8,128)(2,1)S(1)}, u32[]{:S(2)}, u32[]{:S(2)}) async-start(bf16[16,4,128,128]{3,2,1,0:T(8,128)(2,1)} %copy.110), calls=%async_computation.1 | async-start | bytes 4194304 | tf_op jit(solution)/shard_map/all_to_all | solution.py:104
  60.1 1.8 pad_maximum_fusion
  63.4 31.7 %all-to-all-done.1 = bf16[16,4,128,128]{3,2,1,0:T(8,128)(2,1)S(1)} async-done(((bf16[16,4,128,128]{3,2,1,0:T(8,128)(2,1)}), bf16[16,4,128,128]{3,2,1,0:T(8,128)(2,1)S(1)}, u32[]{:S(2)}, u32[]{:S(2)}) %all-to-all-start.1) | async-done | bytes 2097184 | tf_op jit(solution)/shard_map/all_to_all | solution.py:104
  95.0 10.2 %all-to-all-start = ((bf16[16,4,128,128]{3,2,1,0:T(8,128)(2,1)}), bf16[16,4,128,128]{3,2,1,0:T(8,128)(2,1)}, u32[]{:S(2)}, u32[]{:S(2)}) async-start(bf16[16,4,128,128]{3,2,1,0:T(8,128)(2,1)} %copy.105), calls=%async_computation | async-start | bytes 4194304 | tf_op jit(solution)/shard_map/all_to_all | solution.py:103
  114.5 1.8 gather_fusion.15
  116.2 43.3 %all-to-all-done = bf16[16,4,128,128]{3,2,1,0:T(8,128)(2,1)} async-done(((bf16[16,4,128,128]{3,2,1,0:T(8,128)(2,1)}), bf16[16,4,128,128]{3,2,1,0:T(8,128)(2,1)}, u32[]{:S(2)}, u32[]{:S(2)}) %all-to-all-start) | async-done | bytes 2097184 | tf_op jit(solution)/shard_map/all_to_all | solution.py:103
  159.5 1.7 slice_bitcast_fusion.7
  162.6 1.8 gather_fusion.14
  165.1 1.8 gather_fusion.13
  172.1 4.8 %bitcast_reduce_fusion.1 = (f32[4,512]{1,0:T(4,128)S(1)}, f32[4,8,128,512]{3,2,1,0:T(8,128)}) fusion(pred[4,8]{1,0:T(4,128)(4,1)} %not.7, bf16[4,512,128,1]{2,1,3,0:T(8,128)(2,1)S(1)} %bitcast.160, bf16[1,8,128,128]{3,2,1,0:T(8,128)(2,1)S(1)} %get-tuple-element.81, bf16[1,8,128,128]{3,2,1,0:T(8,128)(2,1)S(1)} %get-tuple-element.79, ...), kind=kOutput, calls=%fused_computation.23 | convolution fusion | flops 544733184 | bytes 9969696 | tf_op jit(solution)/shard_map/grd,gikd->grik/dot_general | solution.py:122
  176.9 3.9 %bitcast_reduce_fusion = (f32[4,512]{1,0:T(4,128)S(1)}, f32[4,16,128,512]{3,2,1,0:T(8,128)S(1)}) fusion(pred[4,16]{1,0:T(4,128)(4,1)S(1)} %fusion.49, bf16[16,4,128,128]{3,2,0,1:T(8,128)(2,1)} %all-gather.3.cloned.1.call-done, bf16[4,512,128,1]{2,1,3,0:T(8,128)(2,1)S(1)} %bitcast.161), kind=kOutput, calls=%fused_computation.17 | convolution fusion | flops 1086322688 | bytes 19406912 | tf_op jit(solution)/shard_map/grd,ngkd->grnk/dot_general | solution.py:66
  181.3 1.8 fusion.7
  183.1 3.8 %fusion.1 = f32[4,512]{1,0:T(4,128)S(1)} fusion(f32[4,16,128,512]{3,2,1,0:T(8,128)S(1)} %get-tuple-element.99, f32[4,512]{1,0:T(4,128)S(1)} %get-tuple-element.58, pred[4,16]{1,0:T(4,128)(4,1)S(1)} %fusion.49), kind=kLoop, calls=%fused_computation.20 | loop fusion | flops 16775168 | bytes 16793664 | tf_op jit(solution)/shard_map/reduce_sum | solution.py:19
  186.9 4.1 %fusion.12 = f32[4,512,128]{2,1,0:T(8,128)} fusion(f32[4,8,128,512]{3,2,1,0:T(8,128)S(1)} %copy-done.1, f32[4,512]{1,0:T(4,128)S(1)} %get-tuple-element.10, pred[4,8]{1,0:T(4,128)(4,1)S(1)} %copy-done.5, bf16[1,8,128,128]{3,2,1,0:T(8,128)(2,1)S(1)} %get-tuple-element.80, bf16[1,8,128,128]{3,2,1,0:T(8,128)(2,1)S(1)} %get-tuple-element.78, ...), kind=kOutput, calls=%fused_computation.35 | convolution fusion | flops 546832384 | bytes 10493984 | tf_op jit(solution)/shard_map/grnk,gnkd->grd/dot_general | solution.py:20
  191.0 28.4 %all-gather.5.cloned.1.call-done = bf16[16,4,128,128]{3,2,0,1:T(8,128)(2,1)} async-done(((bf16[1,4,128,128]{3,2,0,1:T(8,128)(2,1)}), bf16[16,4,128,128]{3,2,0,1:T(8,128)(2,1)}) %all-gather.5.cloned.1.call-update) | async-done | bytes 2097168 | tf_op jit(solution)/shard_map/all_gather | solution.py:62
  219.5 8.8 %fusion.25 = f32[4,512,128]{2,1,0:T(8,128)S(1)} fusion(bf16[16,4,128,128]{3,2,0,1:T(8,128)(2,1)} %all-gather.5.cloned.1.call-done, f32[4,16,128,512]{3,2,1,0:T(8,128)} %copy-done, f32[4,512]{1,0:T(4,128)S(1)} %get-tuple-element.58, pred[4,16]{1,0:T(4,128)(4,1)S(1)} %fusion.49, f32[4,512]{1,0:T(4,128)S(1)} %get-tuple-element.9, ...), kind=kOutput, calls=%fused_computation.44 | convolution fusion | flops 1091043328 | bytes 19947584 | tf_op jit(solution)/shard_map/grnk,ngkd->grd/dot_general | solution.py:20
  229.5 9.1 %convolution_convert_fusion = bf16[128,4096]{1,0:T(8,128)(2,1)} fusion(bf16[128,2048]{0,1:T(8,128)(2,1)S(1)} %bitcast.162, bf16[2048,4096]{1,0:T(8,128)(2,1)} %param.13), kind=kOutput, calls=%fused_computation.30 | convolution fusion | flops 2148007936 | bytes 18350080 | tf_op jit(solution)/shard_map/dot_general | solution.py:135
  238.6 7.5 %reduce-scatter.2.cloned.1.call-done = bf16[128,2048]{1,0:T(8,128)(2,1)} async-done(((bf16[128,4096]{1,0:T(8,128)(2,1)}), bf16[128,2048]{1,0:T(8,128)(2,1)}) %reduce-scatter.2.cloned.1.call-update) | async-done | bytes 524304 | tf_op jit(solution)/shard_map/reduce_scatter | solution.py:136
  (96 shorter events, 45.6 us)
Async XLA Ops:
  13.3 21.7 %copy-start.2 = (bf16[8,128,512]{1,2,0:T(8,128)(2,1)}, bf16[8,128,512]{1,2,0:T(8,128)(2,1)S(1)}, u32[]{:S(2)}) copy-start(bf16[8,128,512]{1,2,0:T(8,128)(2,1)S(1)} %copy.84) | copy-start | bytes 3145732
  41.1 54.0 %all-to-all-start.1 = ((bf16[16,4,128,128]{3,2,1,0:T(8,128)(2,1)}), bf16[16,4,128,128]{3,2,1,0:T(8,128)(2,1)S(1)}, u32[]{:S(2)}, u32[]{:S(2)}) async-start(bf16[16,4,128,128]{3,2,1,0:T(8,128)(2,1)} %copy.110), calls=%async_computation.1 | async-start | bytes 4194304 | tf_op jit(solution)/shard_map/all_to_all | solution.py:104
  49.4 57.6 %copy-start.4 = (s32[4,8]{1,0:T(4,128)S(1)}, s32[4,8]{1,0:T(4,128)}, u32[]{:S(2)}) copy-start(s32[4,8]{1,0:T(4,128)} %param.14) | copy-start | bytes 388
  49.4 127.5 %all-gather.3.cloned.1.call-start = ((), (), s32[]{:S(2)}) async-start(), calls=%async_computation.3 | async-start | bytes 2228224 | tf_op jit(solution)/shard_map/all_gather | solution.py:61
  95.0 64.5 %all-to-all-start = ((bf16[16,4,128,128]{3,2,1,0:T(8,128)(2,1)}), bf16[16,4,128,128]{3,2,1,0:T(8,128)(2,1)}, u32[]{:S(2)}, u32[]{:S(2)}) async-start(bf16[16,4,128,128]{3,2,1,0:T(8,128)(2,1)} %copy.105), calls=%async_computation | async-start | bytes 4194304 | tf_op jit(solution)/shard_map/all_to_all | solution.py:103
  105.2 114.2 %all-gather.5.cloned.1.call-start = ((), (), s32[]{:S(2)}) async-start(), calls=%async_computation.4 | async-start | bytes 2228224 | tf_op jit(solution)/shard_map/all_gather | solution.py:62
  106.0 140.1 %reduce-scatter.2.cloned.1.call-start = ((), (), s32[]{:S(2)}) async-start(), calls=%async_computation.5 | async-start | bytes 1572864 | tf_op jit(solution)/shard_map/reduce_scatter | solution.py:136
  176.9 4.0 %copy-start.3 = (f32[4,512,128]{1,2,0:T(8,128)S(1)}, f32[4,512,128]{1,2,0:T(8,128)}, u32[]{:S(2)}) copy-start(f32[4,512,128]{1,2,0:T(8,128)} %get-tuple-element.97) | copy-start | bytes 3145732
  176.9 4.2 %copy-start.5 = (pred[4,8]{1,0:T(4,128)(4,1)S(1)}, pred[4,8]{1,0:T(4,128)(4,1)}, u32[]{:S(2)}) copy-start(pred[4,8]{1,0:T(4,128)(4,1)} %not.7) | copy-start | bytes 100
  176.9 4.3 %copy-start.1 = (f32[4,8,128,512]{3,2,1,0:T(8,128)S(1)}, f32[4,8,128,512]{3,2,1,0:T(8,128)}, u32[]{:S(2)}) copy-start(f32[4,8,128,512]{3,2,1,0:T(8,128)} %get-tuple-element.95) | copy-start | bytes 25165828
  180.9 6.0 %copy-start = (f32[4,16,128,512]{3,2,1,0:T(8,128)}, f32[4,16,128,512]{3,2,1,0:T(8,128)S(1)}, u32[]{:S(2)}) copy-start(f32[4,16,128,512]{3,2,1,0:T(8,128)S(1)} %get-tuple-element.99) | copy-start | bytes 50331652
  219.5 8.8 %copy-start.6 = (f32[4,512,128]{2,1,0:T(8,128)S(1)}, f32[4,512,128]{2,1,0:T(8,128)}, u32[]{:S(2)}) copy-start(f32[4,512,128]{2,1,0:T(8,128)} %fusion.12) | copy-start | bytes 3145732
Sparse Core Ops, SparseCore 0:
  60.3 96.1 all-gather.2
  159.2 60.2 all-gather.4
  238.7 7.2 reduce-scatter.1
where the time goes:
time: 254 us; the launch traced here: 253 us
  waiting for transfers between devices  112 us (44%)
  local copies, waits for them, and re-layouts  42.4 us (17%)
  matrix products  33.1 us (13%)
  other arithmetic  26.1 us (10%)
  between operations  20.9 us (8%)
  starting transfers between devices  18.6 us (7%)
    all_to_all x1, waiting for transfers between devices, per_device(): lax.all_to_all(send_keys, 'ctx', split_axis=0, concat_axis=0, tiled=True)  43.3 us
    all_to_all x1, waiting for transfers between devices, per_device(): lax.all_to_all(send_values, 'ctx', split_axis=0, concat_axis=0, tiled=True)  31.7 us
    all_gather x1, waiting for transfers between devices, per_device(): piece_values = lax.all_gather(slot_values, 'ctx', axis=0, tiled=True)  28.4 us
    dot_general x3, matrix products, absorb(): jnp.einsum(form, weights.astype(jnp.bfloat16), values_tile, preferred_ele...  13.9 us
    all_to_all x1, starting transfers between devices, per_device(): lax.all_to_all(send_keys, 'ctx', split_axis=0, concat_axis=0, tiled=True)  10.2 us
    dot_general x1, matrix products, per_device(): terms = jnp.dot(attended, out_weight, preferred_element_type=jnp.float32)  9.1 us
    another operation x5, other arithmetic, per_device(): jnp.stack([jnp.take(value_local[:, :, group_index, :], source_round[group...  8.71 us
    all_to_all x1, starting transfers between devices, per_device(): lax.all_to_all(send_values, 'ctx', split_axis=0, concat_axis=0, tiled=True)  8.31 us
  transfers between devices with their start and end apart: 5, of which 4 were waited for; matrix products, arithmetic and copies ran while one was open for 19% of the time, Pallas kernels for 0%

commit v1 on v0

v1 whole, which is shorter than its diff:
```python
import functools
import math

import jax
import jax.numpy as jnp
import numpy as np
from jax import lax
from jax.experimental import pallas as pl
from jax.experimental.pallas import tpu as pltpu
from jax.sharding import PartitionSpec as P

H = 32
KVH = 8
HD = 128
NEGATIVE = -1e30
SCALE = HD ** (-0.5) * math.log2(math.e)
MESH = pl.DeviceIdType.MESH


def send_order(shards):
    high = list(range(shards // 2, shards))
    low = list(range(1, shards // 2))
    order = [0]
    for place in range(shards // 2):
        order.append(high[place])
        if place < len(low):
            order.append(low[place])
    steps = shards.bit_length() - 1
    weights = np.cumsum(np.arange(2, steps + 2))
    ends = np.floor((shards - 1) * weights / (weights[-1] + 1)).astype(int)
    ends[-1] = shards - 1
    bounds = [1] + [int(end) + 1 for end in ends]
    return order, bounds


def gather_bits(shards, swap):
    bits = [1 << place for place in reversed(range(shards.bit_length() - 1))]
    if swap:
        bits[-1], bits[-2] = bits[-2], bits[-1]
    return bits


def flipped(index, offset):
    bit = 1
    result = index
    while bit <= offset:
        if offset & bit:
            result = result + bit * (1 - 2 * ((index // bit) % 2))
        bit *= 2
    return result


def kernel(
    shards, heads, index_ref, bias_ref, q_ref, k_ref, v_ref, w_hbm, out_ref,
    qt, acc, top, total, send, recv, vert_k, vert_v, weight, att, part, part_in,
    send_sem, recv_sem, vs_send, vs_recv, w_sem, h_send, h_recv,
):
    groups = qt.shape[0]
    rounds, block = k_ref.shape[0], k_ref.shape[1]
    per = q_ref.shape[1] // (groups * HD)
    width = out_ref.shape[1]
    tile = part.shape[3]
    tiles = width // tile
    me = lax.axis_index("ctx")
    head = lax.axis_index("head")
    order, bounds = send_order(shards)
    steps = shards.bit_length() - 1
    bits_k, bits_v = gather_bits(shards, False), gather_bits(shards, True)

    w_copy = pltpu.make_async_copy(w_hbm, weight, w_sem)
    w_copy.start()

    barrier = pltpu.get_barrier_semaphore()
    for offset in range(1, shards):
        pl.semaphore_signal(
            barrier, inc=1, device_id=(flipped(me, offset), head), device_id_type=MESH
        )
    for offset in range(1, heads):
        pl.semaphore_signal(
            barrier, inc=1, device_id=(me, lax.rem(head + offset, heads)), device_id_type=MESH
        )

    def gather_copy(step, which):
        buffer = (vert_k, vert_v)[which]
        bit = (bits_k, bits_v)[which][step]
        size = 1 << step
        return pltpu.make_async_remote_copy(
            src_ref=buffer.at[pl.ds(0, size)],
            dst_ref=buffer.at[pl.ds(size, size)],
            send_sem=vs_send.at[step, which],
            recv_sem=vs_recv.at[step, which],
            device_id=(flipped(me, bit), head),
            device_id_type=MESH,
        )

    def slash_copy(place, offset):
        return pltpu.make_async_remote_copy(
            src_ref=send.at[place],
            dst_ref=recv.at[place],
            send_sem=send_sem.at[place],
            recv_sem=recv_sem.at[place],
            device_id=(flipped(me, offset), head),
            device_id_type=MESH,
        )

    def fill(target, place):
        for group in range(groups):
            at = index_ref[group, place]
            columns = slice(group * HD, (group + 1) * HD)
            target[place, group, 0] = k_ref[at, :, columns]
            target[place, group, 1] = v_ref[at, :, columns]

    def start_wave(wave):
        for place in range(bounds[wave], bounds[wave + 1]):
            slash_copy(place, order[place]).start()

    for group in range(groups):
        at = index_ref[group, shards]
        columns = slice(group * HD, (group + 1) * HD)
        vert_k[0, group] = k_ref[at, :, columns]
        vert_v[0, group] = v_ref[at, :, columns]

    pl.semaphore_wait(barrier, shards - 1 + heads - 1)
    for which in range(2):
        gather_copy(0, which).start()

    def fill_send(place, carry):
        fill(send, place)
        return carry

    lax.fori_loop(bounds[0], bounds[1], fill_send, 0)
    start_wave(0)
    lax.fori_loop(bounds[1], shards, fill_send, 0)
    fill(recv, 0)

    for group in range(groups):
        for one in range(per):
            start = (group * per + one) * HD
            rows = q_ref[:, start : start + HD].astype(jnp.float32)
            qt[group, :, one * block : (one + 1) * block] = rows.T.astype(jnp.bfloat16)

    columns_q = per * block
    causal = (
        lax.broadcasted_iota(jnp.int32, (block, columns_q), 0)
        <= lax.broadcasted_iota(jnp.int32, (block, columns_q), 1) % block
    )

    def weigh(values_tile, weights):
        return lax.dot_general(
            values_tile,
            weights.astype(jnp.bfloat16),
            (((0,), (0,)), ((), ())),
            preferred_element_type=jnp.float32,
        )

    for group in range(groups):
        columns = slice(group * HD, (group + 1) * HD)
        scores = (
            jnp.dot(
                k_ref[rounds - 1, :, columns], qt[group], preferred_element_type=jnp.float32
            )
            * SCALE
        )
        scores = jnp.where(causal, scores, NEGATIVE)
        peak = jnp.max(scores, axis=0, keepdims=True)
        weights = jnp.exp2(scores - peak)
        top[group] = peak
        total[group] = jnp.sum(weights, axis=0, keepdims=True)
        acc[group] = weigh(v_ref[rounds - 1, :, columns], weights)

    def absorb(group, keys_tile, values_tile, bias):
        scores = (
            jnp.dot(keys_tile, qt[group], preferred_element_type=jnp.float32) * SCALE + bias
        )
        before = top[group]
        peak = jnp.maximum(before, jnp.max(scores, axis=0, keepdims=True))
        weights = jnp.exp2(scores - peak)
        shrink = jnp.exp2(before - peak)
        top[group] = peak
        total[group] = total[group] * shrink + jnp.sum(weights, axis=0, keepdims=True)
        acc[group] = acc[group] * shrink + weigh(values_tile, weights)

    def absorb_vertical(low, high, shift):
        def body(at, carry):
            place, group = low + at // groups, at % groups
            absorb(
                group,
                vert_k[place, group],
                vert_v[place + shift, group],
                bias_ref[group, place],
            )
            return carry

        lax.fori_loop(0, (high - low) * groups, body, 0)

    def absorb_slash_at(place):
        def body(group, carry):
            absorb(
                group, recv[place, group, 0], recv[place, group, 1], bias_ref[group, shards + place]
            )
            return carry

        lax.fori_loop(0, groups, body, 0)

    def absorb_wave(wave):
        def body(place, carry):
            slash_copy(place, 1).wait_recv()
            absorb_slash_at(place)
            return carry

        lax.fori_loop(bounds[wave], bounds[wave + 1], body, 0)

    absorb_slash_at(0)
    absorb_vertical(0, 1, 0)
    quarter = shards // 4
    for step in range(steps):
        for which in range(2):
            gather_copy(step, which).wait_recv()
        if step < steps - 1:
            for which in range(2):
                gather_copy(step + 1, which).start()
            start_wave(step + 1)
        if step < steps - 2:
            absorb_vertical(1 << step, 2 << step, 0)
        if step == steps - 1:
            absorb_vertical(quarter, 2 * quarter, quarter)
            absorb_vertical(2 * quarter, 3 * quarter, -quarter)
            absorb_vertical(3 * quarter, 4 * quarter, 0)
        if step >= 1:
            absorb_wave(step - 1)
    absorb_wave(steps - 1)

    for group in range(groups):
        for one in range(per):
            columns = slice(one * block, (one + 1) * block)
            scaled = acc[group, :, columns] / total[group, :, columns]
            start = (group * per + one) * HD
            att[:, start : start + HD] = scaled.T.astype(jnp.bfloat16)
    w_copy.wait()

    def project(owner, at):
        start = pl.multiple_of(owner * width + at * tile, tile)
        return jnp.dot(
            att[...], weight[:, pl.ds(start, tile)], preferred_element_type=jnp.float32
        )

    def head_copy(offset, at):
        return pltpu.make_async_remote_copy(
            src_ref=part.at[offset - 1, at],
            dst_ref=part_in.at[offset - 1, at],
            send_sem=h_send.at[offset - 1, at],
            recv_sem=h_recv.at[offset - 1, at],
            device_id=(me, lax.rem(head + offset, heads)),
            device_id_type=MESH,
        )

    for offset in range(1, heads):

        def give(at, carry, offset=offset):
            part[offset - 1, at] = project(lax.rem(head + offset, heads), at).astype(jnp.bfloat16)
            head_copy(offset, at).start()
            return carry

        lax.fori_loop(0, tiles, give, 0)

    def keep(at, carry):
        result = project(head, at)
        for offset in range(1, heads):
            head_copy(offset, at).wait_recv()
            result = result + part_in[offset - 1, at].astype(jnp.float32)
        start = pl.multiple_of(at * tile, tile)
        out_ref[:, pl.ds(start, tile)] = result.astype(jnp.bfloat16)
        return carry

    lax.fori_loop(0, tiles, keep, 0)

    for step in range(steps):
        for which in range(2):
            gather_copy(step, which).wait_send()

    def sent(place, carry):
        slash_copy(place, 1).wait_send()
        return carry

    lax.fori_loop(1, shards, sent, 0)
    for offset in range(1, heads):
        for at in range(tiles):
            head_copy(offset, at).wait_send()


def per_device(shards, heads, queries, keys, values, out_weight, vertical, slash):
    me = lax.axis_index("ctx")
    groups = vertical.shape[0]
    rounds = keys.shape[0]
    block = queries.shape[0]
    per = H // KVH
    width = out_weight.shape[1] // heads
    tile = min(512, width)
    last_base = (rounds - 1) * shards

    order, _ = send_order(shards)
    partner = me ^ jnp.asarray(order, jnp.int32)
    residue_s = slash % shards
    wanted = (partner - me) % shards
    matching = residue_s[:, None, :] == wanted[None, :, None]
    chosen = jnp.sum(jnp.where(matching, slash[:, None, :], 0), axis=2)
    slash_round = (last_base + partner[None, :] - chosen) // shards
    holding = vertical % shards == me
    vertical_round = jnp.sum(jnp.where(holding, vertical // shards, 0), axis=1)
    index = jnp.concatenate([slash_round, vertical_round[:, None]], axis=1).astype(jnp.int32)

    bits = gather_bits(shards, False)
    flips = [sum(b for i, b in enumerate(bits) if (p >> i) & 1) for p in range(shards)]
    source = me ^ jnp.asarray(flips, jnp.int32)
    has_vertical = jnp.any((vertical % shards)[:, None, :] == source[None, :, None], axis=2)
    back = (me - partner) % shards
    slash_blocks = last_base + me - slash
    repeated = jnp.any(slash_blocks[:, :, None] == vertical[:, None, :], axis=2)
    has_slash = jnp.any(
        (residue_s[:, None, :] == back[None, :, None]) & ~repeated[:, None, :], axis=2
    )
    bias = jnp.where(
        jnp.concatenate([has_vertical, has_slash], axis=1), 0.0, NEGATIVE
    ).astype(jnp.float32)

    steps = shards.bit_length() - 1
    smem = pl.BlockSpec(memory_space=pltpu.SMEM)
    vmem = pl.BlockSpec(memory_space=pltpu.VMEM)
    dma = pltpu.SemaphoreType.DMA
    return pl.pallas_call(
        functools.partial(kernel, shards, heads),
        out_shape=jax.ShapeDtypeStruct((block, width), jnp.bfloat16),
        in_specs=[smem, smem, vmem, vmem, vmem, pl.BlockSpec(memory_space=pl.ANY)],
        out_specs=vmem,
        scratch_shapes=[
            pltpu.VMEM((groups, HD, per * block), jnp.bfloat16),
            pltpu.VMEM((groups, HD, per * block), jnp.float32),
            pltpu.VMEM((groups, 1, per * block), jnp.float32),
            pltpu.VMEM((groups, 1, per * block), jnp.float32),
            pltpu.VMEM((shards, groups, 2, block, HD), jnp.bfloat16),
            pltpu.VMEM((shards, groups, 2, block, HD), jnp.bfloat16),
            pltpu.VMEM((shards, groups, block, HD), jnp.bfloat16),
            pltpu.VMEM((shards, groups, block, HD), jnp.bfloat16),
            pltpu.VMEM(out_weight.shape, jnp.bfloat16),
            pltpu.VMEM((block, groups * per * HD), jnp.bfloat16),
            pltpu.VMEM((heads - 1, width // tile, block, tile), jnp.bfloat16),
            pltpu.VMEM((heads - 1, width // tile, block, tile), jnp.bfloat16),
            dma((shards,)),
            dma((shards,)),
            dma((steps, 2)),
            dma((steps, 2)),
            dma,
            dma((heads - 1, width // tile)),
            dma((heads - 1, width // tile)),
        ],
        compiler_params=pltpu.CompilerParams(
            collective_id=0, has_side_effects=True, vmem_limit_bytes=56 * 1024 * 1024
        ),
    )(index, bias, queries, keys, values, out_weight)


def solution(mesh):
    in_specs = (
        P("ctx", "head"),
        P(None, "ctx", "head"),
        P(None, "ctx", "head"),
        P("head", None),
        P("head", None),
        P("head", None),
    )
    return jax.shard_map(
        functools.partial(per_device, mesh.shape["ctx"], mesh.shape["head"]),
        mesh=mesh,
        in_specs=in_specs,
        out_specs=P("ctx", "head"),
        check_vma=False,
    )
```

time: 254 us -> 164 us (0.65)
  Pallas kernels: 0 us -> 157 us
  waiting for transfers between devices: 112 us -> 0 us
  local copies, waits for them, and re-layouts: 42.4 us -> 1.97 us
  matrix products: 33.1 us -> 0 us
  between operations: 20.9 us -> 0.02 us
  other arithmetic: 26.1 us -> 5.37 us
  starting transfers between devices: 18.6 us -> 0 us
    pallas_call x0 -> x1, Pallas kernels: none -> 157 us  [per_device(): pl.pallas_call(functools.partial(kernel, shards, heads), out_shape=jax.Sh...]
    all_to_all x2 -> x0, waiting for transfers between devices: 74.9 us -> none  [the longest x1 43.3 us: per_device(): lax.all_to_all(send_keys, 'ctx', split_axis=0, concat_axis=0, tiled=True)]
    dot_general x7 -> x0, matrix products: 33.1 us -> none  [the longest x3 13.9 us: absorb(): jnp.einsum(form, weights.astype(jnp.bfloat16), values_tile, preferred_ele...]
    all_gather x2 -> x0, waiting for transfers between devices: 28.4 us -> none  [the longest x1 28.4 us: per_device(): piece_values = lax.all_gather(slot_values, 'ctx', axis=0, tiled=True)]
    gather x16 -> x0, local copies, waits for them, and re-layouts: 19.8 us -> none  [the longest x4 5.88 us: per_device(): jnp.take(got_values[:, group_index], anchor[group_index], axis=0)]
    all_to_all x2 -> x0, starting transfers between devices: 18.5 us -> none  [the longest x1 10.2 us: per_device(): lax.all_to_all(send_keys, 'ctx', split_axis=0, concat_axis=0, tiled=True)]
    another operation x10 -> x0, other arithmetic: 13.8 us -> none  [the longest x5 8.71 us: per_device(): jnp.stack([jnp.take(value_local[:, :, group_index, :], source_round[group...]
    slice x13 -> x0, local copies, waits for them, and re-layouts: 9.59 us -> none  [the longest x5 4.49 us: per_device(): key_local[:, :, group_index, :]]
  transfers between devices with their start and end apart: 5 -> 0, of which waited for: 4 -> 0; matrix products, arithmetic and copies ran while one was open for 19% -> 0% of each run, Pallas kernels for 0% -> 0%
where the time goes in v1:
time: 164 us
  Pallas kernels  157 us (96%)
  other arithmetic  5.37 us (3%)
  local copies, waits for them, and re-layouts  1.97 us (1%)
    pallas_call x1, Pallas kernels, per_device(): pl.pallas_call(functools.partial(kernel, shards, heads), out_shape=jax.Sh...  157 us

profile of v1, /device:TPU:0, one launch (start us, length us, event | category | flops | bytes accessed | tf_op | source)
XLA Modules:
  0.0 163.9 jit_solution(10006241547376416067)
XLA Ops:
  0.0 0.7 and_select_fusion
  0.7 0.8 add_select_fusion.1
  1.5 0.1 compare_reduce_fusion.1
  1.6 0.1 copy.10
  1.7 0.7 broadcast_subtract_fusion
  2.4 0.9 compare_reduce_fusion
  3.3 0.1 and_reduce_fusion
  3.4 0.8 select_reduce_fusion
  4.2 0.7 pad_add_fusion.index_ref
  4.8 0.7 add_select_fusion.4.bias_ref
  5.5 156.5 %shard_map.82 = bf16[128,2048]{1,0:T(8,128)(2,1)} custom-call(s32[4,17]{1,0:T(4,128)} %pad_add_fusion.index_ref, f32[4,32]{1,0:T(4,128)} %add_select_fusion.4.bias_ref, bf16[128,2048]{1,0:T(8,128)(2,1)} %q_ref.1, bf16[8,128,512]{2,1,0:T(8,128)(2,1)} %k_ref.1, bf16[8,128,512]{2,1,0:T(8,128)(2,1)} %v_ref.1, bf16[2048,4096]{1,0:T(8,128)(2,1)} %w_hbm.1), custom_call_target="tpu_custom_call" | custom-call | tf_op jit(solution)/shard_map/pallas_call | solution.py:330
  162.0 1.9 %copy.12 = bf16[128,2048]{1,0:T(8,128)(2,1)} copy(bf16[128,2048]{1,0:T(8,128)(2,1)} %shard_map.82) | data formatting | bytes 1048576
  (2 shorter events, 0.0 us)

commit v2 on v1

--- a/solution.py
+++ b/solution.py
@@ -3,7 +3,6 @@
 
 import jax
 import jax.numpy as jnp
-import numpy as np
 from jax import lax
 from jax.experimental import pallas as pl
 from jax.experimental.pallas import tpu as pltpu
@@ -17,20 +16,12 @@
 MESH = pl.DeviceIdType.MESH
 
 
-def send_order(shards):
-    high = list(range(shards // 2, shards))
-    low = list(range(1, shards // 2))
-    order = [0]
-    for place in range(shards // 2):
-        order.append(high[place])
-        if place < len(low):
-            order.append(low[place])
-    steps = shards.bit_length() - 1
-    weights = np.cumsum(np.arange(2, steps + 2))
-    ends = np.floor((shards - 1) * weights / (weights[-1] + 1)).astype(int)
-    ends[-1] = shards - 1
-    bounds = [1] + [int(end) + 1 for end in ends]
-    return order, bounds
+PACE = 1.5
+TOGETHER = 2
+
+
+def send_offset(shards, place):
+    return place // 2 + (place % 2) * (shards // 2)
 
 
 def gather_bits(shards, swap):
@@ -40,18 +31,15 @@
     return bits
 
 
-def flipped(index, offset):
-    bit = 1
+def flipped(shards, index, offset):
     result = index
-    while bit <= offset:
-        if offset & bit:
-            result = result + bit * (1 - 2 * ((index // bit) % 2))
-        bit *= 2
+    for bit in (1 << place for place in range(shards.bit_length() - 1)):
+        result = result + bit * ((offset // bit) % 2) * (1 - 2 * ((index // bit) % 2))
     return result
 
 
 def kernel(
-    shards, heads, index_ref, bias_ref, q_ref, k_ref, v_ref, w_hbm, out_ref,
+    shards, heads, vertical_ref, slash_ref, q_ref, k_ref, v_ref, w_hbm, out_ref,
     qt, acc, top, total, send, recv, vert_k, vert_v, weight, att, part, part_in,
     send_sem, recv_sem, vs_send, vs_recv, w_sem, h_send, h_recv,
 ):
@@ -61,24 +49,45 @@
     width = out_ref.shape[1]
     tile = part.shape[3]
     tiles = width // tile
+    verticals, slashes = vertical_ref.shape[1], slash_ref.shape[1]
+    last_base = (rounds - 1) * shards
     me = lax.axis_index("ctx")
     head = lax.axis_index("head")
-    order, bounds = send_order(shards)
     steps = shards.bit_length() - 1
     bits_k, bits_v = gather_bits(shards, False), gather_bits(shards, True)
-
-    w_copy = pltpu.make_async_copy(w_hbm, weight, w_sem)
-    w_copy.start()
+    ends = [1 + max(1, round((shards - 1) * ((step + 1) / steps) ** PACE)) for step in range(steps)]
 
     barrier = pltpu.get_barrier_semaphore()
     for offset in range(1, shards):
         pl.semaphore_signal(
-            barrier, inc=1, device_id=(flipped(me, offset), head), device_id_type=MESH
+            barrier, inc=1, device_id=(flipped(shards, me, offset), head), device_id_type=MESH
         )
     for offset in range(1, heads):
         pl.semaphore_signal(
             barrier, inc=1, device_id=(me, lax.rem(head + offset, heads)), device_id_type=MESH
         )
+
+    def slash_of(group, residue):
+        chosen = 0
+        for at in range(slashes):
+            offset = slash_ref[group, at]
+            chosen = chosen + jnp.where(offset % shards == residue, offset, 0)
+        return chosen
+
+    def slash_bias(group, place):
+        source = flipped(shards, me, send_offset(shards, place))
+        chosen = slash_of(group, (me - source + shards) % shards)
+        repeated = chosen == 0
+        for at in range(verticals):
+            repeated = repeated | (vertical_ref[group, at] == last_base + me - chosen)
+        return jnp.where(repeated, NEGATIVE, 0.0)
+
+    def vertical_place(group, at, bits):
+        source = vertical_ref[group, at] % shards
+        place = 0
+        for step, bit in enumerate(bits):
+            place = place + (1 << step) * ((source // bit + me // bit) % 2)
+        return place
 
     def gather_copy(step, which):
         buffer = (vert_k, vert_v)[which]
@@ -89,33 +98,34 @@
             dst_ref=buffer.at[pl.ds(size, size)],
             send_sem=vs_send.at[step, which],
             recv_sem=vs_recv.at[step, which],
-            device_id=(flipped(me, bit), head),
+            device_id=(flipped(shards, me, bit), head),
             device_id_type=MESH,
         )
 
-    def slash_copy(place, offset):
+    def slash_copy(place):
         return pltpu.make_async_remote_copy(
             src_ref=send.at[place],
             dst_ref=recv.at[place],
             send_sem=send_sem.at[place],
             recv_sem=recv_sem.at[place],
-            device_id=(flipped(me, offset), head),
+            device_id=(flipped(shards, me, send_offset(shards, place)), head),
             device_id_type=MESH,
         )
 
-    def fill(target, place):
+    def fill(buffer, place):
+        target = flipped(shards, me, send_offset(shards, place))
         for group in range(groups):
-            at = index_ref[group, place]
+            chosen = slash_of(group, (target - me + shards) % shards)
+            at = (last_base + target - chosen) // shards
             columns = slice(group * HD, (group + 1) * HD)
-            target[place, group, 0] = k_ref[at, :, columns]
-            target[place, group, 1] = v_ref[at, :, columns]
-
-    def start_wave(wave):
-        for place in range(bounds[wave], bounds[wave + 1]):
-            slash_copy(place, order[place]).start()
+            buffer[place, group, 0] = k_ref[at, :, columns]
+            buffer[place, group, 1] = v_ref[at, :, columns]
 
     for group in range(groups):
-        at = index_ref[group, shards]
+        at = 0
+        for one in range(verticals):
+            block_at = vertical_ref[group, one]
+            at = at + jnp.where(block_at % shards == me, block_at // shards, 0)
         columns = slice(group * HD, (group + 1) * HD)
         vert_k[0, group] = k_ref[at, :, columns]
         vert_v[0, group] = v_ref[at, :, columns]
@@ -124,13 +134,14 @@
     for which in range(2):
         gather_copy(0, which).start()
 
-    def fill_send(place, carry):
+    def launch(place, carry):
         fill(send, place)
-        return carry
-
-    lax.fori_loop(bounds[0], bounds[1], fill_send, 0)
-    start_wave(0)
-    lax.fori_loop(bounds[1], shards, fill_send, 0)
+        slash_copy(place).start()
+        return carry
+
+    lax.fori_loop(1, ends[0], launch, 0)
+    w_copy = pltpu.make_async_copy(w_hbm, weight, w_sem)
+    w_copy.start()
     fill(recv, 0)
 
     for group in range(groups):
@@ -169,9 +180,9 @@
         acc[group] = weigh(v_ref[rounds - 1, :, columns], weights)
 
     def absorb(group, keys_tile, values_tile, bias):
-        scores = (
-            jnp.dot(keys_tile, qt[group], preferred_element_type=jnp.float32) * SCALE + bias
-        )
+        scores = jnp.dot(keys_tile, qt[group], preferred_element_type=jnp.float32) * SCALE
+        if bias is not None:
+            scores = scores + bias
         before = top[group]
         peak = jnp.maximum(before, jnp.max(scores, axis=0, keepdims=True))
         weights = jnp.exp2(scores - peak)
@@ -180,55 +191,39 @@
         total[group] = total[group] * shrink + jnp.sum(weights, axis=0, keepdims=True)
         acc[group] = acc[group] * shrink + weigh(values_tile, weights)
 
-    def absorb_vertical(low, high, shift):
-        def body(at, carry):
-            place, group = low + at // groups, at % groups
-            absorb(
-                group,
-                vert_k[place, group],
-                vert_v[place + shift, group],
-                bias_ref[group, place],
-            )
-            return carry
-
-        lax.fori_loop(0, (high - low) * groups, body, 0)
-
-    def absorb_slash_at(place):
-        def body(group, carry):
-            absorb(
-                group, recv[place, group, 0], recv[place, group, 1], bias_ref[group, shards + place]
-            )
-            return carry
-
-        lax.fori_loop(0, groups, body, 0)
-
-    def absorb_wave(wave):
-        def body(place, carry):
-            slash_copy(place, 1).wait_recv()
-            absorb_slash_at(place)
-            return carry
-
-        lax.fori_loop(bounds[wave], bounds[wave + 1], body, 0)
-
-    absorb_slash_at(0)
-    absorb_vertical(0, 1, 0)
-    quarter = shards // 4
+    def absorb_slash(place):
+        for group in range(groups):
+            absorb(group, recv[place, group, 0], recv[place, group, 1], slash_bias(group, place))
+
+    def absorb_vertical(turn, carry):
+        for group in range(groups):
+            keys_tile, values_tile = [], []
+            for one in range(TOGETHER):
+                at = turn * TOGETHER + one
+                keys_tile.append(vert_k[vertical_place(group, at, bits_k), group])
+                values_tile.append(vert_v[vertical_place(group, at, bits_v), group])
+            absorb(group, jnp.concatenate(keys_tile), jnp.concatenate(values_tile), None)
+        return carry
+
+    def slash_arrival(place, carry):
+        slash_copy(place).wait_recv()
+        absorb_slash(place)
+        return carry
+
+    absorb_slash(0)
+    done = 1
     for step in range(steps):
         for which in range(2):
             gather_copy(step, which).wait_recv()
         if step < steps - 1:
             for which in range(2):
                 gather_copy(step + 1, which).start()
-            start_wave(step + 1)
-        if step < steps - 2:
-            absorb_vertical(1 << step, 2 << step, 0)
-        if step == steps - 1:
-            absorb_vertical(quarter, 2 * quarter, quarter)
-            absorb_vertical(2 * quarter, 3 * quarter, -quarter)
-            absorb_vertical(3 * quarter, 4 * quarter, 0)
-        if step >= 1:
-            absorb_wave(step - 1)
-    absorb_wave(steps - 1)
+            lax.fori_loop(ends[step], ends[step + 1], launch, 0)
+        if 1 <= step < steps - 1:
+            lax.fori_loop(done, ends[step - 1], slash_arrival, 0)
+            done = ends[step - 1]
+    lax.fori_loop(0, verticals // TOGETHER, absorb_vertical, 0)
+    lax.fori_loop(done, shards, slash_arrival, 0)
 
     for group in range(groups):
         for one in range(per):
@@ -279,7 +274,7 @@
             gather_copy(step, which).wait_send()
 
     def sent(place, carry):
-        slash_copy(place, 1).wait_send()
+        slash_copy(place).wait_send()
         return carry
 
     lax.fori_loop(1, shards, sent, 0)
@@ -289,40 +284,11 @@
 
 
 def per_device(shards, heads, queries, keys, values, out_weight, vertical, slash):
-    me = lax.axis_index("ctx")
     groups = vertical.shape[0]
-    rounds = keys.shape[0]
     block = queries.shape[0]
     per = H // KVH
     width = out_weight.shape[1] // heads
     tile = min(512, width)
-    last_base = (rounds - 1) * shards
-
-    order, _ = send_order(shards)
-    partner = me ^ jnp.asarray(order, jnp.int32)
-    residue_s = slash % shards
-    wanted = (partner - me) % shards
-    matching = residue_s[:, None, :] == wanted[None, :, None]
-    chosen = jnp.sum(jnp.where(matching, slash[:, None, :], 0), axis=2)
-    slash_round = (last_base + partner[None, :] - chosen) // shards
-    holding = vertical % shards == me
-    vertical_round = jnp.sum(jnp.where(holding, vertical // shards, 0), axis=1)
-    index = jnp.concatenate([slash_round, vertical_round[:, None]], axis=1).astype(jnp.int32)
-
-    bits = gather_bits(shards, False)
-    flips = [sum(b for i, b in enumerate(bits) if (p >> i) & 1) for p in range(shards)]
-    source = me ^ jnp.asarray(flips, jnp.int32)
-    has_vertical = jnp.any((vertical % shards)[:, None, :] == source[None, :, None], axis=2)
-    back = (me - partner) % shards
-    slash_blocks = last_base + me - slash
-    repeated = jnp.any(slash_blocks[:, :, None] == vertical[:, None, :], axis=2)
-    has_slash = jnp.any(
-        (residue_s[:, None, :] == back[None, :, None]) & ~repeated[:, None, :], axis=2
-    )
-    bias = jnp.where(
-        jnp.concatenate([has_vertical, has_slash], axis=1), 0.0, NEGATIVE
-    ).astype(jnp.float32)
-
     steps = shards.bit_length() - 1
     smem = pl.BlockSpec(memory_space=pltpu.SMEM)
     vmem = pl.BlockSpec(memory_space=pltpu.VMEM)
@@ -356,7 +322,7 @@
         compiler_params=pltpu.CompilerParams(
             collective_id=0, has_side_effects=True, vmem_limit_bytes=56 * 1024 * 1024
         ),
-    )(index, bias, queries, keys, values, out_weight)
+    )(vertical, slash, queries, keys, values, out_weight)
 
 
 def solution(mesh):

time: 164 us -> 142 us (0.87)
  Pallas kernels: 157 us -> 140 us
  other arithmetic: 5.37 us -> 0 us
    pallas_call x1, Pallas kernels: 157 us -> 140 us  [per_device(): pl.pallas_call(functools.partial(kernel, shards, heads), out_shape=jax.Sh...]
    select_n x4 -> x0, other arithmetic: 2.17 us -> none  [the longest x1 0.8 us: per_device(): holding = vertical % shards == me]
where the time goes in v2:
time: 142 us
  Pallas kernels  140 us (99%)
  local copies, waits for them, and re-layouts  1.88 us (1%)
    pallas_call x1, Pallas kernels, per_device(): pl.pallas_call(functools.partial(kernel, shards, heads), out_shape=jax.Sh...  140 us

profile of v2, /device:TPU:0, one launch (start us, length us, event | category | flops | bytes accessed | tf_op | source)
XLA Modules:
  0.0 142.0 jit_solution(12356920593311415373)
XLA Ops:
  0.0 140.1 %shard_map.64 = bf16[128,2048]{1,0:T(8,128)(2,1)} custom-call(s32[4,8]{1,0:T(4,128)} %vertical_ref.1, s32[4,8]{1,0:T(4,128)} %slash_ref.1, bf16[128,2048]{1,0:T(8,128)(2,1)} %q_ref.1, bf16[8,128,512]{2,1,0:T(8,128)(2,1)} %k_ref.1, bf16[8,128,512]{2,1,0:T(8,128)(2,1)} %v_ref.1, bf16[2048,4096]{1,0:T(8,128)(2,1)} %w_hbm.1), custom_call_target="tpu_custom_call" | custom-call | tf_op jit(solution)/shard_map/pallas_call | solution.py:296
  140.1 1.9 %copy.8 = bf16[128,2048]{1,0:T(8,128)(2,1)} copy(bf16[128,2048]{1,0:T(8,128)(2,1)} %shard_map.64) | data formatting | bytes 1048576

commit v3 on v2

--- a/solution.py
+++ b/solution.py
@@ -17,6 +17,7 @@
 
 
 PACE = 1.5
+AHEAD = 5
 TOGETHER = 2
 
 
@@ -218,12 +219,23 @@
         if step < steps - 1:
             for which in range(2):
                 gather_copy(step + 1, which).start()
-            lax.fori_loop(ends[step], ends[step + 1], launch, 0)
+            upto = min(ends[step + 1], ends[steps - 2] + 1)
+            lax.fori_loop(ends[step], upto, launch, 0)
         if 1 <= step < steps - 1:
             lax.fori_loop(done, ends[step - 1], slash_arrival, 0)
             done = ends[step - 1]
     lax.fori_loop(0, verticals // TOGETHER, absorb_vertical, 0)
-    lax.fori_loop(done, shards, slash_arrival, 0)
+    ahead = max(AHEAD, upto - done)
+
+    def slash_turn(place, carry):
+        slash_copy(place).wait_recv()
+        launch(place + ahead, carry)
+        absorb_slash(place)
+        return carry
+
+    lax.fori_loop(upto, done + ahead, launch, 0)
+    lax.fori_loop(done, shards - ahead, slash_turn, 0)
+    lax.fori_loop(shards - ahead, shards, slash_arrival, 0)
 
     for group in range(groups):
         for one in range(per):

time: 142 us -> 142 us (level)
  no operation moved by 1% of the time
where the time goes in v3:
time: 142 us
  Pallas kernels  140 us (99%)
  local copies, waits for them, and re-layouts  1.88 us (1%)
    pallas_call x1, Pallas kernels, per_device(): pl.pallas_call(functools.partial(kernel, shards, heads), out_shape=jax.Sh...  140 us

profile of v3, /device:TPU:0, one launch (start us, length us, event | category | flops | bytes accessed | tf_op | source)
XLA Modules:
  0.0 141.9 jit_solution(11822092170262614100)
XLA Ops:
  0.0 140.0 %shard_map.64 = bf16[128,2048]{1,0:T(8,128)(2,1)} custom-call(s32[4,8]{1,0:T(4,128)} %vertical_ref.1, s32[4,8]{1,0:T(4,128)} %slash_ref.1, bf16[128,2048]{1,0:T(8,128)(2,1)} %q_ref.1, bf16[8,128,512]{2,1,0:T(8,128)(2,1)} %k_ref.1, bf16[8,128,512]{2,1,0:T(8,128)(2,1)} %v_ref.1, bf16[2048,4096]{1,0:T(8,128)(2,1)} %w_hbm.1), custom_call_target="tpu_custom_call" | custom-call | tf_op jit(solution)/shard_map/pallas_call | solution.py:308
  140.0 1.9 %copy.8 = bf16[128,2048]{1,0:T(8,128)(2,1)} copy(bf16[128,2048]{1,0:T(8,128)(2,1)} %shard_map.64) | data formatting | bytes 1048576
